TPU v7x, 32 devices: a whole 2x2x4 slice. The times are simulated.
32 devices in a mesh: rot: 8 (over z, y), fft: 4 (over x, core).
Axes of the slice: x: 2, y: 2, z: 4, core: 2. Of those that a mesh axis runs over, the one named last changes fastest.
Arguments:
- receptor: bfloat16 [2, 11, 128, 128, 128], P(None, None, 'fft'), may hold values from -6 to 6, as said below
- ligand_grids: bfloat16 [32, 11, 32, 1024], P(None, None, 'fft'), may hold values from -8 to 8
- rot_index: int32 [48], P('rot'), parts along dimension 0, may hold values from 0 to 31
Outputs:
- scores: float32 [48, 128, 128, 128], P('rot', 'fft'), parts along dimension 0
- best: float32 [48], P('rot'), parts along dimension 0
There are 8 independent parts, one for each index of `rot`. A program takes and returns all parts, laid end to end along the dimension named above; an argument that names none is the same for every part. Nothing has to cross between parts.
Inputs may be any that keep to these rules, and one draw needn't show every extreme that they name: The receptor spectra are those of real grids: in every channel the entry at frequency (-kz, -kx, -ky), taken modulo 128 along each dimension, is the complex conjugate of the entry at (kz, kx, ky).
All inputs are finite; a program needn't handle non-finite values.
Results may differ from a plain program's by a relative error of at most 0.0003.
Values may be sent and summed in bfloat16 or wider, within the bound.
A program may use at most 256 MiB of HBM per device.

v0:
```python
import math
import jax
import jax.numpy as jnp
from jax import lax
from jax.sharding import PartitionSpec as P

TRIPLE = lax.Precision.HIGH


def phase_table(row_index, col_index, length):
    turns = row_index[:, None] * col_index[None, :] % length
    angle = turns.astype(jnp.float32) * (2.0 * math.pi / length)
    return (jnp.cos(angle), jnp.sin(angle))


def split_table(table):
    upper = table.astype(jnp.bfloat16)
    widened = lax.optimization_barrier(upper).astype(jnp.float32)
    return (upper, (table - widened).astype(jnp.bfloat16))


def contract(form, left, right):
    return jnp.einsum(form, left, right, precision=TRIPLE)


def narrow_contract(form, values, table_pair):
    upper = jnp.einsum(form, values, table_pair[0], preferred_element_type=jnp.float32)
    lower = jnp.einsum(form, values, table_pair[1], preferred_element_type=jnp.float32)
    return upper + lower


def shards(receptor, ligand_grids, rot_index):
    groups = lax.axis_size("fft")
    slab_depth = receptor.shape[2]
    length = receptor.shape[3]
    channels = receptor.shape[1]
    box_cells = ligand_grids.shape[2] * groups
    rotations = rot_index.shape[0]
    freq_slab = lax.axis_index("fft") * slab_depth + jnp.arange(slab_depth, dtype=jnp.int32)
    freq_all = jnp.arange(length, dtype=jnp.int32)
    cos_box, sin_box = phase_table(jnp.arange(box_cells, dtype=jnp.int32), freq_all, length)
    cos_full, sin_full = phase_table(freq_all, freq_all, length)
    inverse_volume = 1.0 / float(length) ** 3
    chosen = jnp.take(ligand_grids, rot_index, axis=0)
    empty = jnp.zeros((rotations, channels, slab_depth, ligand_grids.shape[3]), jnp.float32)
    planes = lax.all_gather(chosen, "fft", axis=2, tiled=True)
    plane_index = jnp.arange(planes.shape[2], dtype=jnp.int32)
    cos_depth, sin_depth = phase_table(plane_index, freq_slab, length)
    slab_real = narrow_contract("rczp,zk->rckp", planes, split_table(cos_depth))
    slab_imag = (empty, empty)[1] - narrow_contract("rczp,zk->rckp", planes, split_table(sin_depth))

    def ligand_product(one_real, one_imag):
        grid_real = one_real.reshape(channels, slab_depth, box_cells, box_cells)
        grid_imag = one_imag.reshape(channels, slab_depth, box_cells, box_cells)
        half_real = contract("ckxy,yb->ckxb", grid_real, cos_box) + contract(
            "ckxy,yb->ckxb", grid_imag, sin_box
        )
        half_imag = contract("ckxy,yb->ckxb", grid_imag, cos_box) - contract(
            "ckxy,yb->ckxb", grid_real, sin_box
        )
        spec_real = contract("ckxb,xa->ckab", half_real, cos_box) + contract(
            "ckxb,xa->ckab", half_imag, sin_box
        )
        spec_imag = contract("ckxb,xa->ckab", half_imag, cos_box) - contract(
            "ckxb,xa->ckab", half_real, sin_box
        )
        prod_real = jnp.sum(receptor[0] * spec_real + receptor[1] * spec_imag, axis=0)
        prod_imag = jnp.sum(receptor[1] * spec_real - receptor[0] * spec_imag, axis=0)
        return (prod_real, prod_imag)

    def inverse_plane(prod_real, prod_imag):
        rows_real = contract("kay,yb->kab", prod_real, cos_full) - contract(
            "kay,yb->kab", prod_imag, sin_full
        )
        rows_imag = contract("kay,yb->kab", prod_imag, cos_full) + contract(
            "kay,yb->kab", prod_real, sin_full
        )
        grid_real = contract("kab,ax->kxb", rows_real, cos_full) - contract(
            "kab,ax->kxb", rows_imag, sin_full
        )
        grid_imag = contract("kab,ax->kxb", rows_imag, cos_full) + contract(
            "kab,ax->kxb", rows_real, sin_full
        )
        return (grid_real, grid_imag)

    def one_rotation(single):
        prod_real, prod_imag = ligand_product(single[0], single[1])
        return inverse_plane(prod_real, prod_imag)

    planes_real, planes_imag = lax.map(one_rotation, (slab_real, slab_imag))
    part_real = lax.all_to_all(planes_real, "fft", split_axis=2, concat_axis=1, tiled=True)
    part_imag = lax.all_to_all(planes_imag, "fft", split_axis=2, concat_axis=1, tiled=True)
    field = contract("rkxy,kz->rxyz", part_real, cos_full) - contract(
        "rkxy,kz->rxyz", part_imag, sin_full
    )
    scores = field * inverse_volume
    best = lax.pmin(jnp.min(scores, axis=(1, 2, 3)), "fft")
    return (scores, best)


def solution(mesh):
    placed = (P(None, None, "fft", None, None), P(None, None, "fft", None), P("rot"))
    return jax.shard_map(
        shards,
        mesh=mesh,
        in_specs=placed,
        out_specs=(P("rot", "fft", None, None), P("rot")),
        check_vma=False,
    )
```

profile of v0, /device:TPU:0, one launch (start us, length us, event | category | flops | bytes accessed | tf_op | source)
XLA Modules:
  0.0 1411.9 jit_solution(3870738557738267873)
XLA Ops:
  13.2 29.4 %copy.31 = bf16[2,11,32,128,128]{3,4,2,1,0:T(8,128)(2,1)} copy(bf16[2,11,32,128,128]{4,3,2,1,0:T(8,128)(2,1)} %param.5) | data formatting | bytes 46137344
  42.5 8.5 all-gather.2.cloned.1.call-done
  56.3 4.7 add_bitcast_fusion.1
  65.7 996.6 %while.14 = (s32[]{:T(128)}, f32[6,32,128,128]{3,1,0,2:T(8,128)}, f32[6,32,128,128]{3,1,0,2:T(8,128)}, bf16[2,11,32,128,128]{3,4,2,1,0:T(8,128)(2,1)}, f32[6,11,...) while((s32[]{:T(128)}, f32[6,32,128,128]{3,1,0,2:T(8,128)}, ...), condition=%wide.region_3.4_spmd.clone.clone, body=%wide.region_0.3_spmd.clone.clone.sunk | while | flops 8833138688 | bytes 390595392 | solution.py:90
  71.0 7.6 fusion.291
  83.7 7.0 convolution_add_fusion.4
  90.7 21.8 %fusion.292 = f32[11,32,128,128]{3,2,1,0:T(8,128)} fusion(f32[11,32,32,128]{3,2,1,0:T(8,128)S(1)} %convolution_add_fusion.4), kind=kOutput, calls=%fused_computation.48.clone.1 | convolution fusion | flops 1107353600 | bytes 28835840 | tf_op jit(solution)/shard_map/while/body/eval_jaxpr/ckxb,xa->ckab/dot_general | solution.py:23
  112.4 21.3 %fusion.293 = f32[11,32,128,128]{3,2,1,0:T(8,128)} fusion(f32[11,32,32,128]{3,2,1,0:T(8,128)S(1)} %convolution_add_fusion.4), kind=kOutput, calls=%fused_computation.58.clone.1 | convolution fusion | flops 1107353600 | bytes 28835840 | tf_op jit(solution)/shard_map/while/body/eval_jaxpr/ckxb,xa->ckab/dot_general | solution.py:23
  138.8 21.2 %fusion.295 = f32[11,32,128,128]{3,2,1,0:T(8,128)} fusion(f32[11,32,32,128]{3,2,1,0:T(8,128)S(1)} %convolution_subtract_fusion.4), kind=kOutput, calls=%fused_computation.50.clone.1 | convolution fusion | flops 1107353600 | bytes 28835840 | tf_op jit(solution)/shard_map/while/body/eval_jaxpr/ckxb,xa->ckab/dot_general | solution.py:23
  160.0 37.3 %fusion.296 = (f32[32,128,128]{1,2,0:T(8,128)}, f32[32,128,128]{1,2,0:T(8,128)S(1)}) fusion(f32[11,32,128,128]{3,2,1,0:T(8,128)} %fusion.292, bf16[2,11,32,128,128]{3,4,2,1,0:T(8,128)(2,1)} %get-tuple-element.251, f32[11,32,128,128]{3,2,1,0:T(8,128)} %fusion.293, f32[11,32,128,128]{3,2,1,0:T(8,128)} %fusion.295, f32[11,32,32,128]{3,2,1,0:T(8,128)} %copy-done), kind=kOutput, calls=%fused_computation.12.clone.1 | convolution fusion | flops 1175511040 | bytes 102236160 | tf_op jit(solution)/shard_map/while/body/eval_jaxpr/ckxb,xa->ckab/dot_general | solution.py:23
  235.7 7.6 fusion.291
  248.4 7.0 convolution_add_fusion.4
  255.4 21.4 %fusion.292 = f32[11,32,128,128]{3,2,1,0:T(8,128)} fusion(f32[11,32,32,128]{3,2,1,0:T(8,128)S(1)} %convolution_add_fusion.4), kind=kOutput, calls=%fused_computation.48.clone.1 | convolution fusion | flops 1107353600 | bytes 28835840 | tf_op jit(solution)/shard_map/while/body/eval_jaxpr/ckxb,xa->ckab/dot_general | solution.py:23
  276.9 21.6 %fusion.293 = f32[11,32,128,128]{3,2,1,0:T(8,128)} fusion(f32[11,32,32,128]{3,2,1,0:T(8,128)S(1)} %convolution_add_fusion.4), kind=kOutput, calls=%fused_computation.58.clone.1 | convolution fusion | flops 1107353600 | bytes 28835840 | tf_op jit(solution)/shard_map/while/body/eval_jaxpr/ckxb,xa->ckab/dot_general | solution.py:23
  303.6 21.2 %fusion.295 = f32[11,32,128,128]{3,2,1,0:T(8,128)} fusion(f32[11,32,32,128]{3,2,1,0:T(8,128)S(1)} %convolution_subtract_fusion.4), kind=kOutput, calls=%fused_computation.50.clone.1 | convolution fusion | flops 1107353600 | bytes 28835840 | tf_op jit(solution)/shard_map/while/body/eval_jaxpr/ckxb,xa->ckab/dot_general | solution.py:23
  324.8 37.2 %fusion.296 = (f32[32,128,128]{1,2,0:T(8,128)}, f32[32,128,128]{1,2,0:T(8,128)S(1)}) fusion(f32[11,32,128,128]{3,2,1,0:T(8,128)} %fusion.292, bf16[2,11,32,128,128]{3,4,2,1,0:T(8,128)(2,1)} %get-tuple-element.251, f32[11,32,128,128]{3,2,1,0:T(8,128)} %fusion.293, f32[11,32,128,128]{3,2,1,0:T(8,128)} %fusion.295, f32[11,32,32,128]{3,2,1,0:T(8,128)} %copy-done), kind=kOutput, calls=%fused_computation.12.clone.1 | convolution fusion | flops 1175511040 | bytes 102236160 | tf_op jit(solution)/shard_map/while/body/eval_jaxpr/ckxb,xa->ckab/dot_general | solution.py:23
  400.3 7.6 fusion.291
  413.0 7.0 convolution_add_fusion.4
  420.0 21.7 %fusion.292 = f32[11,32,128,128]{3,2,1,0:T(8,128)} fusion(f32[11,32,32,128]{3,2,1,0:T(8,128)S(1)} %convolution_add_fusion.4), kind=kOutput, calls=%fused_computation.48.clone.1 | convolution fusion | flops 1107353600 | bytes 28835840 | tf_op jit(solution)/shard_map/while/body/eval_jaxpr/ckxb,xa->ckab/dot_general | solution.py:23
  441.7 21.3 %fusion.293 = f32[11,32,128,128]{3,2,1,0:T(8,128)} fusion(f32[11,32,32,128]{3,2,1,0:T(8,128)S(1)} %convolution_add_fusion.4), kind=kOutput, calls=%fused_computation.58.clone.1 | convolution fusion | flops 1107353600 | bytes 28835840 | tf_op jit(solution)/shard_map/while/body/eval_jaxpr/ckxb,xa->ckab/dot_general | solution.py:23
  468.1 21.2 %fusion.295 = f32[11,32,128,128]{3,2,1,0:T(8,128)} fusion(f32[11,32,32,128]{3,2,1,0:T(8,128)S(1)} %convolution_subtract_fusion.4), kind=kOutput, calls=%fused_computation.50.clone.1 | convolution fusion | flops 1107353600 | bytes 28835840 | tf_op jit(solution)/shard_map/while/body/eval_jaxpr/ckxb,xa->ckab/dot_general | solution.py:23
  489.3 37.3 %fusion.296 = (f32[32,128,128]{1,2,0:T(8,128)}, f32[32,128,128]{1,2,0:T(8,128)S(1)}) fusion(f32[11,32,128,128]{3,2,1,0:T(8,128)} %fusion.292, bf16[2,11,32,128,128]{3,4,2,1,0:T(8,128)(2,1)} %get-tuple-element.251, f32[11,32,128,128]{3,2,1,0:T(8,128)} %fusion.293, f32[11,32,128,128]{3,2,1,0:T(8,128)} %fusion.295, f32[11,32,32,128]{3,2,1,0:T(8,128)} %copy-done), kind=kOutput, calls=%fused_computation.12.clone.1 | convolution fusion | flops 1175511040 | bytes 102236160 | tf_op jit(solution)/shard_map/while/body/eval_jaxpr/ckxb,xa->ckab/dot_general | solution.py:23
  565.0 7.6 fusion.291
  577.7 7.0 convolution_add_fusion.4
  584.7 21.4 %fusion.292 = f32[11,32,128,128]{3,2,1,0:T(8,128)} fusion(f32[11,32,32,128]{3,2,1,0:T(8,128)S(1)} %convolution_add_fusion.4), kind=kOutput, calls=%fused_computation.48.clone.1 | convolution fusion | flops 1107353600 | bytes 28835840 | tf_op jit(solution)/shard_map/while/body/eval_jaxpr/ckxb,xa->ckab/dot_general | solution.py:23
  606.2 21.6 %fusion.293 = f32[11,32,128,128]{3,2,1,0:T(8,128)} fusion(f32[11,32,32,128]{3,2,1,0:T(8,128)S(1)} %convolution_add_fusion.4), kind=kOutput, calls=%fused_computation.58.clone.1 | convolution fusion | flops 1107353600 | bytes 28835840 | tf_op jit(solution)/shard_map/while/body/eval_jaxpr/ckxb,xa->ckab/dot_general | solution.py:23
  632.8 21.2 %fusion.295 = f32[11,32,128,128]{3,2,1,0:T(8,128)} fusion(f32[11,32,32,128]{3,2,1,0:T(8,128)S(1)} %convolution_subtract_fusion.4), kind=kOutput, calls=%fused_computation.50.clone.1 | convolution fusion | flops 1107353600 | bytes 28835840 | tf_op jit(solution)/shard_map/while/body/eval_jaxpr/ckxb,xa->ckab/dot_general | solution.py:23
  654.1 37.2 %fusion.296 = (f32[32,128,128]{1,2,0:T(8,128)}, f32[32,128,128]{1,2,0:T(8,128)S(1)}) fusion(f32[11,32,128,128]{3,2,1,0:T(8,128)} %fusion.292, bf16[2,11,32,128,128]{3,4,2,1,0:T(8,128)(2,1)} %get-tuple-element.251, f32[11,32,128,128]{3,2,1,0:T(8,128)} %fusion.293, f32[11,32,128,128]{3,2,1,0:T(8,128)} %fusion.295, f32[11,32,32,128]{3,2,1,0:T(8,128)} %copy-done), kind=kOutput, calls=%fused_computation.12.clone.1 | convolution fusion | flops 1175511040 | bytes 102236160 | tf_op jit(solution)/shard_map/while/body/eval_jaxpr/ckxb,xa->ckab/dot_general | solution.py:23
  729.6 7.6 fusion.291
  742.3 7.0 convolution_add_fusion.4
  749.3 21.7 %fusion.292 = f32[11,32,128,128]{3,2,1,0:T(8,128)} fusion(f32[11,32,32,128]{3,2,1,0:T(8,128)S(1)} %convolution_add_fusion.4), kind=kOutput, calls=%fused_computation.48.clone.1 | convolution fusion | flops 1107353600 | bytes 28835840 | tf_op jit(solution)/shard_map/while/body/eval_jaxpr/ckxb,xa->ckab/dot_general | solution.py:23
  771.0 21.3 %fusion.293 = f32[11,32,128,128]{3,2,1,0:T(8,128)} fusion(f32[11,32,32,128]{3,2,1,0:T(8,128)S(1)} %convolution_add_fusion.4), kind=kOutput, calls=%fused_computation.58.clone.1 | convolution fusion | flops 1107353600 | bytes 28835840 | tf_op jit(solution)/shard_map/while/body/eval_jaxpr/ckxb,xa->ckab/dot_general | solution.py:23
  797.4 21.2 %fusion.295 = f32[11,32,128,128]{3,2,1,0:T(8,128)} fusion(f32[11,32,32,128]{3,2,1,0:T(8,128)S(1)} %convolution_subtract_fusion.4), kind=kOutput, calls=%fused_computation.50.clone.1 | convolution fusion | flops 1107353600 | bytes 28835840 | tf_op jit(solution)/shard_map/while/body/eval_jaxpr/ckxb,xa->ckab/dot_general | solution.py:23
  818.6 37.3 %fusion.296 = (f32[32,128,128]{1,2,0:T(8,128)}, f32[32,128,128]{1,2,0:T(8,128)S(1)}) fusion(f32[11,32,128,128]{3,2,1,0:T(8,128)} %fusion.292, bf16[2,11,32,128,128]{3,4,2,1,0:T(8,128)(2,1)} %get-tuple-element.251, f32[11,32,128,128]{3,2,1,0:T(8,128)} %fusion.293, f32[11,32,128,128]{3,2,1,0:T(8,128)} %fusion.295, f32[11,32,32,128]{3,2,1,0:T(8,128)} %copy-done), kind=kOutput, calls=%fused_computation.12.clone.1 | convolution fusion | flops 1175511040 | bytes 102236160 | tf_op jit(solution)/shard_map/while/body/eval_jaxpr/ckxb,xa->ckab/dot_general | solution.py:23
  894.3 7.6 fusion.291
  907.0 7.0 convolution_add_fusion.4
  914.0 21.4 %fusion.292 = f32[11,32,128,128]{3,2,1,0:T(8,128)} fusion(f32[11,32,32,128]{3,2,1,0:T(8,128)S(1)} %convolution_add_fusion.4), kind=kOutput, calls=%fused_computation.48.clone.1 | convolution fusion | flops 1107353600 | bytes 28835840 | tf_op jit(solution)/shard_map/while/body/eval_jaxpr/ckxb,xa->ckab/dot_general | solution.py:23
  935.4 21.6 %fusion.293 = f32[11,32,128,128]{3,2,1,0:T(8,128)} fusion(f32[11,32,32,128]{3,2,1,0:T(8,128)S(1)} %convolution_add_fusion.4), kind=kOutput, calls=%fused_computation.58.clone.1 | convolution fusion | flops 1107353600 | bytes 28835840 | tf_op jit(solution)/shard_map/while/body/eval_jaxpr/ckxb,xa->ckab/dot_general | solution.py:23
  962.1 21.2 %fusion.295 = f32[11,32,128,128]{3,2,1,0:T(8,128)} fusion(f32[11,32,32,128]{3,2,1,0:T(8,128)S(1)} %convolution_subtract_fusion.4), kind=kOutput, calls=%fused_computation.50.clone.1 | convolution fusion | flops 1107353600 | bytes 28835840 | tf_op jit(solution)/shard_map/while/body/eval_jaxpr/ckxb,xa->ckab/dot_general | solution.py:23
  983.3 37.2 %fusion.296 = (f32[32,128,128]{1,2,0:T(8,128)}, f32[32,128,128]{1,2,0:T(8,128)S(1)}) fusion(f32[11,32,128,128]{3,2,1,0:T(8,128)} %fusion.292, bf16[2,11,32,128,128]{3,4,2,1,0:T(8,128)(2,1)} %get-tuple-element.251, f32[11,32,128,128]{3,2,1,0:T(8,128)} %fusion.293, f32[11,32,128,128]{3,2,1,0:T(8,128)} %fusion.295, f32[11,32,32,128]{3,2,1,0:T(8,128)} %copy-done), kind=kOutput, calls=%fused_computation.12.clone.1 | convolution fusion | flops 1175511040 | bytes 102236160 | tf_op jit(solution)/shard_map/while/body/eval_jaxpr/ckxb,xa->ckab/dot_general | solution.py:23
  1062.4 147.4 %all_to_all.36 = f32[6,32,128,128]{3,1,0,2:T(8,128)} all-to-all(f32[6,32,128,128]{3,1,0,2:T(8,128)} %get-tuple-element.92), channel_id=1, replica_groups=mesh['rot'=8,'fft'=4] {'fft'}, dimensions={2} | all-to-all | bytes 25165824 | tf_op jit(solution)/shard_map/all_to_all | solution.py:92
  1209.8 6.3 all-to-all-start
  1216.1 20.0 %copy.38 = f32[6,4,32,32,128]{4,3,2,1,0:T(8,128)} copy(f32[6,4,32,32,128]{4,2,0,3,1:T(8,128)} %bitcast.214) | data formatting | bytes 25165824 | tf_op jit(solution)/shard_map/all_to_all | solution.py:92
  1236.1 22.9 %fusion.134 = f32[6,32,128,128]{3,2,1,0:T(8,128)} fusion(f32[6,128,32,128]{3,2,1,0:T(8,128)} %bitcast.213), kind=kOutput, calls=%fused_computation.135 | convolution fusion | flops 2416148480 | bytes 25165824 | tf_op jit(solution)/shard_map/rkxy,kz->rxyz/dot_general | solution.py:23
  1258.9 95.3 %all-to-all-done = f32[6,32,128,128]{3,1,0,2:T(8,128)} async-done(((f32[6,32,128,128]{3,1,0,2:T(8,128)}), f32[6,32,128,128]{3,1,0,2:T(8,128)}, u32[]{:S(2)}, u32[]{:S(2)}) %all-to-all-start) | async-done | bytes 12582944 | tf_op jit(solution)/shard_map/all_to_all | solution.py:91
  1354.2 20.0 %copy.34 = f32[6,4,32,32,128]{4,3,2,1,0:T(8,128)} copy(f32[6,4,32,32,128]{4,2,0,3,1:T(8,128)} %bitcast.12) | data formatting | bytes 25165824 | tf_op jit(solution)/shard_map/all_to_all | solution.py:91
  1374.2 24.5 %fusion.198 = (f32[6]{0:T(128)S(1)}, f32[6,32,128,128]{3,2,1,0:T(8,128)}) fusion(f32[6,32,128,128]{3,2,1,0:T(8,128)} %fusion.134, f32[6,128,32,128]{3,2,1,0:T(8,128)} %bitcast.212), kind=kOutput, calls=%fused_computation.205 | convolution fusion | flops 2425585664 | bytes 37748760 | tf_op jit(solution)/shard_map/rkxy,kz->rxyz/dot_general | solution.py:23
  1398.6 6.2 pmin.7
  (238 shorter events, 304.9 us)
Async XLA Ops:
  7.2 43.9 %all-gather.2.cloned.1.call-start = ((), (), s32[]{:S(2)}) async-start(), calls=%async_computation.2 | async-start | bytes 5406720 | tf_op jit(solution)/shard_map/all_gather | solution.py:46
  90.7 43.1 %slice-start.2 = ((s8[5767168]{0:T(1024)(128)(4,1)}), s8[4194304]{0:T(1024)(128)(4,1)S(1)}, s32[]{:S(2)}) async-start(s8[5767168]{0:T(1024)(128)(4,1)} %bitcast.210), calls=%async_computation.5 | async-start | bytes 8388608 | tf_op jit(solution)/shard_map/while
  90.7 45.6 %slice-start = ((s8[5767168]{0:T(1024)(128)(4,1)}), s8[4194304]{0:T(1024)(128)(4,1)S(1)}, s32[]{:S(2)}) async-start(s8[5767168]{0:T(1024)(128)(4,1)} %bitcast.208), calls=%async_computation.3 | async-start | bytes 8388608 | tf_op jit(solution)/shard_map/while
  112.4 21.3 %slice-start.3 = ((s8[5767168]{0:T(1024)(128)(4,1)}), s8[1572864]{0:T(1024)(128)(4,1)S(1)}, s32[]{:S(2)}) async-start(s8[5767168]{0:T(1024)(128)(4,1)} %bitcast.210), calls=%async_computation.6 | async-start | bytes 3145728 | tf_op jit(solution)/shard_map/while
  112.4 23.9 %slice-start.1 = ((s8[5767168]{0:T(1024)(128)(4,1)}), s8[1572864]{0:T(1024)(128)(4,1)S(1)}, s32[]{:S(2)}) async-start(s8[5767168]{0:T(1024)(128)(4,1)} %bitcast.208), calls=%async_computation.4 | async-start | bytes 3145728 | tf_op jit(solution)/shard_map/while
  138.8 21.2 %copy-start = (f32[11,32,32,128]{3,2,1,0:T(8,128)}, f32[11,32,32,128]{3,2,1,0:T(8,128)S(1)}, u32[]{:S(2)}) copy-start(f32[11,32,32,128]{3,2,1,0:T(8,128)S(1)} %convolution_subtract_fusion.4) | copy-start | bytes 17301508 | tf_op jit(solution)/shard_map/while
  199.3 5.7 copy-start.1
  203.0 5.9 copy-start.2
  214.0 6.8 copy-start.3
  255.4 43.1 %slice-start.2 = ((s8[5767168]{0:T(1024)(128)(4,1)}), s8[4194304]{0:T(1024)(128)(4,1)S(1)}, s32[]{:S(2)}) async-start(s8[5767168]{0:T(1024)(128)(4,1)} %bitcast.210), calls=%async_computation.5 | async-start | bytes 8388608 | tf_op jit(solution)/shard_map/while
  255.4 45.6 %slice-start = ((s8[5767168]{0:T(1024)(128)(4,1)}), s8[4194304]{0:T(1024)(128)(4,1)S(1)}, s32[]{:S(2)}) async-start(s8[5767168]{0:T(1024)(128)(4,1)} %bitcast.208), calls=%async_computation.3 | async-start | bytes 8388608 | tf_op jit(solution)/shard_map/while
  276.9 21.6 %slice-start.3 = ((s8[5767168]{0:T(1024)(128)(4,1)}), s8[1572864]{0:T(1024)(128)(4,1)S(1)}, s32[]{:S(2)}) async-start(s8[5767168]{0:T(1024)(128)(4,1)} %bitcast.210), calls=%async_computation.6 | async-start | bytes 3145728 | tf_op jit(solution)/shard_map/while
  276.9 24.2 %slice-start.1 = ((s8[5767168]{0:T(1024)(128)(4,1)}), s8[1572864]{0:T(1024)(128)(4,1)S(1)}, s32[]{:S(2)}) async-start(s8[5767168]{0:T(1024)(128)(4,1)} %bitcast.208), calls=%async_computation.4 | async-start | bytes 3145728 | tf_op jit(solution)/shard_map/while
  303.5 21.2 %copy-start = (f32[11,32,32,128]{3,2,1,0:T(8,128)}, f32[11,32,32,128]{3,2,1,0:T(8,128)S(1)}, u32[]{:S(2)}) copy-start(f32[11,32,32,128]{3,2,1,0:T(8,128)S(1)} %convolution_subtract_fusion.4) | copy-start | bytes 17301508 | tf_op jit(solution)/shard_map/while
  364.0 5.7 copy-start.1
  367.7 5.9 copy-start.2
  378.5 6.8 copy-start.3
  420.0 43.0 %slice-start.2 = ((s8[5767168]{0:T(1024)(128)(4,1)}), s8[4194304]{0:T(1024)(128)(4,1)S(1)}, s32[]{:S(2)}) async-start(s8[5767168]{0:T(1024)(128)(4,1)} %bitcast.210), calls=%async_computation.5 | async-start | bytes 8388608 | tf_op jit(solution)/shard_map/while
  420.0 45.6 %slice-start = ((s8[5767168]{0:T(1024)(128)(4,1)}), s8[4194304]{0:T(1024)(128)(4,1)S(1)}, s32[]{:S(2)}) async-start(s8[5767168]{0:T(1024)(128)(4,1)} %bitcast.208), calls=%async_computation.3 | async-start | bytes 8388608 | tf_op jit(solution)/shard_map/while
  441.7 21.3 %slice-start.3 = ((s8[5767168]{0:T(1024)(128)(4,1)}), s8[1572864]{0:T(1024)(128)(4,1)S(1)}, s32[]{:S(2)}) async-start(s8[5767168]{0:T(1024)(128)(4,1)} %bitcast.210), calls=%async_computation.6 | async-start | bytes 3145728 | tf_op jit(solution)/shard_map/while
  441.7 23.9 %slice-start.1 = ((s8[5767168]{0:T(1024)(128)(4,1)}), s8[1572864]{0:T(1024)(128)(4,1)S(1)}, s32[]{:S(2)}) async-start(s8[5767168]{0:T(1024)(128)(4,1)} %bitcast.208), calls=%async_computation.4 | async-start | bytes 3145728 | tf_op jit(solution)/shard_map/while
  468.1 21.2 %copy-start = (f32[11,32,32,128]{3,2,1,0:T(8,128)}, f32[11,32,32,128]{3,2,1,0:T(8,128)S(1)}, u32[]{:S(2)}) copy-start(f32[11,32,32,128]{3,2,1,0:T(8,128)S(1)} %convolution_subtract_fusion.4) | copy-start | bytes 17301508 | tf_op jit(solution)/shard_map/while
  528.6 5.7 copy-start.1
  532.3 5.9 copy-start.2
  543.3 6.8 copy-start.3
  584.7 43.1 %slice-start.2 = ((s8[5767168]{0:T(1024)(128)(4,1)}), s8[4194304]{0:T(1024)(128)(4,1)S(1)}, s32[]{:S(2)}) async-start(s8[5767168]{0:T(1024)(128)(4,1)} %bitcast.210), calls=%async_computation.5 | async-start | bytes 8388608 | tf_op jit(solution)/shard_map/while
  584.7 45.6 %slice-start = ((s8[5767168]{0:T(1024)(128)(4,1)}), s8[4194304]{0:T(1024)(128)(4,1)S(1)}, s32[]{:S(2)}) async-start(s8[5767168]{0:T(1024)(128)(4,1)} %bitcast.208), calls=%async_computation.3 | async-start | bytes 8388608 | tf_op jit(solution)/shard_map/while
  606.2 21.6 %slice-start.3 = ((s8[5767168]{0:T(1024)(128)(4,1)}), s8[1572864]{0:T(1024)(128)(4,1)S(1)}, s32[]{:S(2)}) async-start(s8[5767168]{0:T(1024)(128)(4,1)} %bitcast.210), calls=%async_computation.6 | async-start | bytes 3145728 | tf_op jit(solution)/shard_map/while
  606.2 24.2 %slice-start.1 = ((s8[5767168]{0:T(1024)(128)(4,1)}), s8[1572864]{0:T(1024)(128)(4,1)S(1)}, s32[]{:S(2)}) async-start(s8[5767168]{0:T(1024)(128)(4,1)} %bitcast.208), calls=%async_computation.4 | async-start | bytes 3145728 | tf_op jit(solution)/shard_map/while
  632.8 21.2 %copy-start = (f32[11,32,32,128]{3,2,1,0:T(8,128)}, f32[11,32,32,128]{3,2,1,0:T(8,128)S(1)}, u32[]{:S(2)}) copy-start(f32[11,32,32,128]{3,2,1,0:T(8,128)S(1)} %convolution_subtract_fusion.4) | copy-start | bytes 17301508 | tf_op jit(solution)/shard_map/while
  693.3 5.7 copy-start.1
  697.0 5.9 copy-start.2
  707.8 6.8 copy-start.3
  749.3 43.0 %slice-start.2 = ((s8[5767168]{0:T(1024)(128)(4,1)}), s8[4194304]{0:T(1024)(128)(4,1)S(1)}, s32[]{:S(2)}) async-start(s8[5767168]{0:T(1024)(128)(4,1)} %bitcast.210), calls=%async_computation.5 | async-start | bytes 8388608 | tf_op jit(solution)/shard_map/while
  749.3 45.6 %slice-start = ((s8[5767168]{0:T(1024)(128)(4,1)}), s8[4194304]{0:T(1024)(128)(4,1)S(1)}, s32[]{:S(2)}) async-start(s8[5767168]{0:T(1024)(128)(4,1)} %bitcast.208), calls=%async_computation.3 | async-start | bytes 8388608 | tf_op jit(solution)/shard_map/while
  771.0 21.3 %slice-start.3 = ((s8[5767168]{0:T(1024)(128)(4,1)}), s8[1572864]{0:T(1024)(128)(4,1)S(1)}, s32[]{:S(2)}) async-start(s8[5767168]{0:T(1024)(128)(4,1)} %bitcast.210), calls=%async_computation.6 | async-start | bytes 3145728 | tf_op jit(solution)/shard_map/while
  771.0 23.9 %slice-start.1 = ((s8[5767168]{0:T(1024)(128)(4,1)}), s8[1572864]{0:T(1024)(128)(4,1)S(1)}, s32[]{:S(2)}) async-start(s8[5767168]{0:T(1024)(128)(4,1)} %bitcast.208), calls=%async_computation.4 | async-start | bytes 3145728 | tf_op jit(solution)/shard_map/while
  797.4 21.2 %copy-start = (f32[11,32,32,128]{3,2,1,0:T(8,128)}, f32[11,32,32,128]{3,2,1,0:T(8,128)S(1)}, u32[]{:S(2)}) copy-start(f32[11,32,32,128]{3,2,1,0:T(8,128)S(1)} %convolution_subtract_fusion.4) | copy-start | bytes 17301508 | tf_op jit(solution)/shard_map/while
  861.6 5.9 copy-start.2
  872.6 6.8 copy-start.3
  914.0 43.1 %slice-start.2 = ((s8[5767168]{0:T(1024)(128)(4,1)}), s8[4194304]{0:T(1024)(128)(4,1)S(1)}, s32[]{:S(2)}) async-start(s8[5767168]{0:T(1024)(128)(4,1)} %bitcast.210), calls=%async_computation.5 | async-start | bytes 8388608 | tf_op jit(solution)/shard_map/while
  914.0 45.6 %slice-start = ((s8[5767168]{0:T(1024)(128)(4,1)}), s8[4194304]{0:T(1024)(128)(4,1)S(1)}, s32[]{:S(2)}) async-start(s8[5767168]{0:T(1024)(128)(4,1)} %bitcast.208), calls=%async_computation.3 | async-start | bytes 8388608 | tf_op jit(solution)/shard_map/while
  935.4 21.6 %slice-start.3 = ((s8[5767168]{0:T(1024)(128)(4,1)}), s8[1572864]{0:T(1024)(128)(4,1)S(1)}, s32[]{:S(2)}) async-start(s8[5767168]{0:T(1024)(128)(4,1)} %bitcast.210), calls=%async_computation.6 | async-start | bytes 3145728 | tf_op jit(solution)/shard_map/while
  935.4 24.2 %slice-start.1 = ((s8[5767168]{0:T(1024)(128)(4,1)}), s8[1572864]{0:T(1024)(128)(4,1)S(1)}, s32[]{:S(2)}) async-start(s8[5767168]{0:T(1024)(128)(4,1)} %bitcast.208), calls=%async_computation.4 | async-start | bytes 3145728 | tf_op jit(solution)/shard_map/while
  962.1 21.2 %copy-start = (f32[11,32,32,128]{3,2,1,0:T(8,128)}, f32[11,32,32,128]{3,2,1,0:T(8,128)S(1)}, u32[]{:S(2)}) copy-start(f32[11,32,32,128]{3,2,1,0:T(8,128)S(1)} %convolution_subtract_fusion.4) | copy-start | bytes 17301508 | tf_op jit(solution)/shard_map/while
  1026.3 5.9 copy-start.2
  1037.1 6.8 copy-start.3
  1209.8 144.4 %all-to-all-start = ((f32[6,32,128,128]{3,1,0,2:T(8,128)}), f32[6,32,128,128]{3,1,0,2:T(8,128)}, u32[]{:S(2)}, u32[]{:S(2)}) async-start(f32[6,32,128,128]{3,1,0,2:T(8,128)} %get-tuple-element.91), calls=%async_computation | async-start | bytes 25165824 | tf_op jit(solution)/shard_map/all_to_all | solution.py:91
  (9 other events, 23.2 us)
Sparse Core Ops, SparseCore 0:
  13.1 37.9 all-gather.1
where the time goes:
time: 1420 us; the launch traced here: 1410 us
  matrix products  921 us (65%)
  local copies, waits for them, and re-layouts  199 us (14%)
  blocking collectives  154 us (11%)
  waiting for transfers between devices  104 us (7%)
  between operations  14.3 us (1%)
    dot_general x98, matrix products, contract(): return jnp.einsum(form, left, right, precision=TRIPLE)  906 us
    all_to_all x1, blocking collectives, shards(): lax.all_to_all(planes_imag, 'fft', split_axis=2, concat_axis=1, tiled=True)  147 us
    all_to_all x1, waiting for transfers between devices, shards(): lax.all_to_all(planes_real, 'fft', split_axis=2, concat_axis=1, tiled=True)  95.3 us
    dynamic_update_slice x18, local copies, waits for them, and re-layouts, shards(): planes_real, planes_imag = lax.map(one_rotation, (slab_real, slab_imag))  57.8 us
    unnamed x3, local copies, waits for them, and re-layouts  29.4 us
  transfers between devices with their start and end apart: 2, of which 2 were waited for; matrix products, arithmetic and copies ran while one was open for 5% of the time, Pallas kernels for 0%

commit v1 on v0

--- a/solution.py
+++ b/solution.py
@@ -88,7 +88,12 @@
         return inverse_plane(prod_real, prod_imag)
 
     planes_real, planes_imag = lax.map(one_rotation, (slab_real, slab_imag))
-    part_real = lax.all_to_all(planes_real, "fft", split_axis=2, concat_axis=1, tiled=True)
+    part_real = jnp.concatenate(
+        lax.all_to_all(
+            jnp.stack(jnp.split(planes_real, lax.axis_size("fft"), axis=2)), "fft", 0, 0
+        ),
+        axis=1,
+    )
     part_imag = lax.all_to_all(planes_imag, "fft", split_axis=2, concat_axis=1, tiled=True)
     field = contract("rkxy,kz->rxyz", part_real, cos_full) - contract(
         "rkxy,kz->rxyz", part_imag, sin_full

time: 1420 us -> 1340 us (0.944)
  blocking collectives: 154 us -> 6.23 us
  waiting for transfers between devices: 104 us -> 225 us
  matrix products: 921 us -> 864 us
    all_to_all x1 -> x0, blocking collectives: 147 us -> none  [shards(): lax.all_to_all(planes_imag, 'fft', split_axis=2, concat_axis=1, tiled=True)]
    all_to_all x1 -> x2, waiting for transfers between devices: 95.3 us -> 217 us  [the longest x1 121 us: shards(): lax.all_to_all(planes_imag, 'fft', split_axis=2, concat_axis=1, tiled=True)]
    dot_general x98, matrix products: 906 us -> 850 us  [contract(): return jnp.einsum(form, left, right, precision=TRIPLE)]
    dynamic_update_slice x18 -> x24, local copies, waits for them, and re-layouts: 57.8 us -> 67.4 us  [shards(): planes_real, planes_imag = lax.map(one_rotation, (slab_real, slab_imag))]
  transfers between devices with their start and end apart: 2 -> 3, of which waited for: 2 -> 3; matrix products, arithmetic and copies ran while one was open for 5% -> 7% of each run, Pallas kernels for 0% -> 0%
where the time goes in v1:
time: 1340 us; the launch traced here: 1330 us
  matrix products  864 us (64%)
  waiting for transfers between devices  225 us (17%)
  local copies, waits for them, and re-layouts  194 us (14%)
  between operations  14.3 us (1%)
    dot_general x98, matrix products, contract(): return jnp.einsum(form, left, right, precision=TRIPLE)  850 us
    all_to_all x1, waiting for transfers between devices, shards(): lax.all_to_all(planes_imag, 'fft', split_axis=2, concat_axis=1, tiled=True)  121 us
    all_to_all x1, waiting for transfers between devices, shards(): lax.all_to_all(jnp.stack(jnp.split(planes_real, lax.axis_size('fft'), axi...  95.5 us
    dynamic_update_slice x24, local copies, waits for them, and re-layouts, shards(): planes_real, planes_imag = lax.map(one_rotation, (slab_real, slab_imag))  67.4 us
    unnamed x3, local copies, waits for them, and re-layouts  29.4 us
  transfers between devices with their start and end apart: 3, of which 3 were waited for; matrix products, arithmetic and copies ran while one was open for 7% of the time, Pallas kernels for 0%

profile of v1, /device:TPU:0, one launch (start us, length us, event | category | flops | bytes accessed | tf_op | source)
XLA Modules:
  0.0 1333.1 jit_solution(7367252410424921784)
XLA Ops:
  13.2 29.4 %copy.33 = bf16[2,11,32,128,128]{3,4,2,1,0:T(8,128)(2,1)} copy(bf16[2,11,32,128,128]{4,3,2,1,0:T(8,128)(2,1)} %param.5) | data formatting | bytes 46137344
  42.5 8.5 all-gather.2.cloned.1.call-done
  51.1 3.8 fusion.162
  56.3 4.7 subtract_bitcast_fusion.1
  61.0 4.7 add_bitcast_fusion.1
  65.7 929.0 %while.14 = (s32[]{:T(128)}, f32[6,32,128,128]{3,2,1,0:T(8,128)}, f32[6,32,128,128]{3,1,0,2:T(8,128)}, bf16[2,11,32,128,128]{3,4,2,1,0:T(8,128)(2,1)}, f32[6,11,...) while((s32[]{:T(128)}, f32[6,32,128,128]{3,2,1,0:T(8,128)}, ...), condition=%wide.region_3.4_spmd.clone.clone, body=%wide.region_0.3_spmd.clone.clone.sunk | while | flops 8833138688 | bytes 365428992 | solution.py:90
  74.8 5.8 fusion.294
  88.2 21.4 %fusion.293 = f32[11,32,128,128]{3,2,1,0:T(8,128)} fusion(f32[11,32,32,128]{3,2,1,0:T(8,128)S(1)} %convolution_add_fusion.4), kind=kOutput, calls=%fused_computation.58.clone.1 | convolution fusion | flops 1107353600 | bytes 28835840 | tf_op jit(solution)/shard_map/while/body/eval_jaxpr/ckxb,xa->ckab/dot_general | solution.py:23
  109.6 21.2 %fusion.292 = f32[11,32,128,128]{3,2,1,0:T(8,128)} fusion(f32[11,32,32,128]{3,2,1,0:T(8,128)S(1)} %convolution_add_fusion.4), kind=kOutput, calls=%fused_computation.48.clone.1 | convolution fusion | flops 1107353600 | bytes 28835840 | tf_op jit(solution)/shard_map/while/body/eval_jaxpr/ckxb,xa->ckab/dot_general | solution.py:23
  130.8 21.6 %fusion.295 = f32[11,32,128,128]{3,2,1,0:T(8,128)} fusion(f32[11,32,32,128]{3,2,1,0:T(8,128)S(1)} %convolution_subtract_fusion.4), kind=kOutput, calls=%fused_computation.50.clone.1 | convolution fusion | flops 1107353600 | bytes 28835840 | tf_op jit(solution)/shard_map/while/body/eval_jaxpr/ckxb,xa->ckab/dot_general | solution.py:23
  152.4 37.2 %fusion.296 = (f32[32,128,128]{1,2,0:T(8,128)}, f32[32,128,128]{1,2,0:T(8,128)S(1)}) fusion(f32[11,32,128,128]{3,2,1,0:T(8,128)} %fusion.292, bf16[2,11,32,128,128]{3,4,2,1,0:T(8,128)(2,1)} %get-tuple-element.255, f32[11,32,128,128]{3,2,1,0:T(8,128)} %fusion.293, f32[11,32,128,128]{3,2,1,0:T(8,128)} %fusion.295, f32[11,32,32,128]{3,2,1,0:T(8,128)} %copy-done), kind=kOutput, calls=%fused_computation.12.clone.1 | convolution fusion | flops 1175511040 | bytes 102236160 | tf_op jit(solution)/shard_map/while/body/eval_jaxpr/ckxb,xa->ckab/dot_general | solution.py:23
  191.7 3.6 convolution_subtract_fusion.5
  229.3 5.8 fusion.294
  242.7 21.4 %fusion.293 = f32[11,32,128,128]{3,2,1,0:T(8,128)} fusion(f32[11,32,32,128]{3,2,1,0:T(8,128)S(1)} %convolution_add_fusion.4), kind=kOutput, calls=%fused_computation.58.clone.1 | convolution fusion | flops 1107353600 | bytes 28835840 | tf_op jit(solution)/shard_map/while/body/eval_jaxpr/ckxb,xa->ckab/dot_general | solution.py:23
  264.0 21.2 %fusion.292 = f32[11,32,128,128]{3,2,1,0:T(8,128)} fusion(f32[11,32,32,128]{3,2,1,0:T(8,128)S(1)} %convolution_add_fusion.4), kind=kOutput, calls=%fused_computation.48.clone.1 | convolution fusion | flops 1107353600 | bytes 28835840 | tf_op jit(solution)/shard_map/while/body/eval_jaxpr/ckxb,xa->ckab/dot_general | solution.py:23
  285.2 21.4 %fusion.295 = f32[11,32,128,128]{3,2,1,0:T(8,128)} fusion(f32[11,32,32,128]{3,2,1,0:T(8,128)S(1)} %convolution_subtract_fusion.4), kind=kOutput, calls=%fused_computation.50.clone.1 | convolution fusion | flops 1107353600 | bytes 28835840 | tf_op jit(solution)/shard_map/while/body/eval_jaxpr/ckxb,xa->ckab/dot_general | solution.py:23
  306.7 37.5 %fusion.296 = (f32[32,128,128]{1,2,0:T(8,128)}, f32[32,128,128]{1,2,0:T(8,128)S(1)}) fusion(f32[11,32,128,128]{3,2,1,0:T(8,128)} %fusion.292, bf16[2,11,32,128,128]{3,4,2,1,0:T(8,128)(2,1)} %get-tuple-element.255, f32[11,32,128,128]{3,2,1,0:T(8,128)} %fusion.293, f32[11,32,128,128]{3,2,1,0:T(8,128)} %fusion.295, f32[11,32,32,128]{3,2,1,0:T(8,128)} %copy-done), kind=kOutput, calls=%fused_computation.12.clone.1 | convolution fusion | flops 1175511040 | bytes 102236160 | tf_op jit(solution)/shard_map/while/body/eval_jaxpr/ckxb,xa->ckab/dot_general | solution.py:23
  383.5 5.8 fusion.294
  396.9 21.6 %fusion.293 = f32[11,32,128,128]{3,2,1,0:T(8,128)} fusion(f32[11,32,32,128]{3,2,1,0:T(8,128)S(1)} %convolution_add_fusion.4), kind=kOutput, calls=%fused_computation.58.clone.1 | convolution fusion | flops 1107353600 | bytes 28835840 | tf_op jit(solution)/shard_map/while/body/eval_jaxpr/ckxb,xa->ckab/dot_general | solution.py:23
  418.5 21.2 %fusion.292 = f32[11,32,128,128]{3,2,1,0:T(8,128)} fusion(f32[11,32,32,128]{3,2,1,0:T(8,128)S(1)} %convolution_add_fusion.4), kind=kOutput, calls=%fused_computation.48.clone.1 | convolution fusion | flops 1107353600 | bytes 28835840 | tf_op jit(solution)/shard_map/while/body/eval_jaxpr/ckxb,xa->ckab/dot_general | solution.py:23
  439.7 21.4 %fusion.295 = f32[11,32,128,128]{3,2,1,0:T(8,128)} fusion(f32[11,32,32,128]{3,2,1,0:T(8,128)S(1)} %convolution_subtract_fusion.4), kind=kOutput, calls=%fused_computation.50.clone.1 | convolution fusion | flops 1107353600 | bytes 28835840 | tf_op jit(solution)/shard_map/while/body/eval_jaxpr/ckxb,xa->ckab/dot_general | solution.py:23
  461.1 37.3 %fusion.296 = (f32[32,128,128]{1,2,0:T(8,128)}, f32[32,128,128]{1,2,0:T(8,128)S(1)}) fusion(f32[11,32,128,128]{3,2,1,0:T(8,128)} %fusion.292, bf16[2,11,32,128,128]{3,4,2,1,0:T(8,128)(2,1)} %get-tuple-element.255, f32[11,32,128,128]{3,2,1,0:T(8,128)} %fusion.293, f32[11,32,128,128]{3,2,1,0:T(8,128)} %fusion.295, f32[11,32,32,128]{3,2,1,0:T(8,128)} %copy-done), kind=kOutput, calls=%fused_computation.12.clone.1 | convolution fusion | flops 1175511040 | bytes 102236160 | tf_op jit(solution)/shard_map/while/body/eval_jaxpr/ckxb,xa->ckab/dot_general | solution.py:23
  537.9 5.8 fusion.294
  551.3 21.4 %fusion.293 = f32[11,32,128,128]{3,2,1,0:T(8,128)} fusion(f32[11,32,32,128]{3,2,1,0:T(8,128)S(1)} %convolution_add_fusion.4), kind=kOutput, calls=%fused_computation.58.clone.1 | convolution fusion | flops 1107353600 | bytes 28835840 | tf_op jit(solution)/shard_map/while/body/eval_jaxpr/ckxb,xa->ckab/dot_general | solution.py:23
  572.7 21.2 %fusion.292 = f32[11,32,128,128]{3,2,1,0:T(8,128)} fusion(f32[11,32,32,128]{3,2,1,0:T(8,128)S(1)} %convolution_add_fusion.4), kind=kOutput, calls=%fused_computation.48.clone.1 | convolution fusion | flops 1107353600 | bytes 28835840 | tf_op jit(solution)/shard_map/while/body/eval_jaxpr/ckxb,xa->ckab/dot_general | solution.py:23
  593.9 21.6 %fusion.295 = f32[11,32,128,128]{3,2,1,0:T(8,128)} fusion(f32[11,32,32,128]{3,2,1,0:T(8,128)S(1)} %convolution_subtract_fusion.4), kind=kOutput, calls=%fused_computation.50.clone.1 | convolution fusion | flops 1107353600 | bytes 28835840 | tf_op jit(solution)/shard_map/while/body/eval_jaxpr/ckxb,xa->ckab/dot_general | solution.py:23
  615.5 37.2 %fusion.296 = (f32[32,128,128]{1,2,0:T(8,128)}, f32[32,128,128]{1,2,0:T(8,128)S(1)}) fusion(f32[11,32,128,128]{3,2,1,0:T(8,128)} %fusion.292, bf16[2,11,32,128,128]{3,4,2,1,0:T(8,128)(2,1)} %get-tuple-element.255, f32[11,32,128,128]{3,2,1,0:T(8,128)} %fusion.293, f32[11,32,128,128]{3,2,1,0:T(8,128)} %fusion.295, f32[11,32,32,128]{3,2,1,0:T(8,128)} %copy-done), kind=kOutput, calls=%fused_computation.12.clone.1 | convolution fusion | flops 1175511040 | bytes 102236160 | tf_op jit(solution)/shard_map/while/body/eval_jaxpr/ckxb,xa->ckab/dot_general | solution.py:23
  692.4 5.8 fusion.294
  705.8 21.4 %fusion.293 = f32[11,32,128,128]{3,2,1,0:T(8,128)} fusion(f32[11,32,32,128]{3,2,1,0:T(8,128)S(1)} %convolution_add_fusion.4), kind=kOutput, calls=%fused_computation.58.clone.1 | convolution fusion | flops 1107353600 | bytes 28835840 | tf_op jit(solution)/shard_map/while/body/eval_jaxpr/ckxb,xa->ckab/dot_general | solution.py:23
  727.2 21.2 %fusion.292 = f32[11,32,128,128]{3,2,1,0:T(8,128)} fusion(f32[11,32,32,128]{3,2,1,0:T(8,128)S(1)} %convolution_add_fusion.4), kind=kOutput, calls=%fused_computation.48.clone.1 | convolution fusion | flops 1107353600 | bytes 28835840 | tf_op jit(solution)/shard_map/while/body/eval_jaxpr/ckxb,xa->ckab/dot_general | solution.py:23
  748.4 21.4 %fusion.295 = f32[11,32,128,128]{3,2,1,0:T(8,128)} fusion(f32[11,32,32,128]{3,2,1,0:T(8,128)S(1)} %convolution_subtract_fusion.4), kind=kOutput, calls=%fused_computation.50.clone.1 | convolution fusion | flops 1107353600 | bytes 28835840 | tf_op jit(solution)/shard_map/while/body/eval_jaxpr/ckxb,xa->ckab/dot_general | solution.py:23
  769.8 37.5 %fusion.296 = (f32[32,128,128]{1,2,0:T(8,128)}, f32[32,128,128]{1,2,0:T(8,128)S(1)}) fusion(f32[11,32,128,128]{3,2,1,0:T(8,128)} %fusion.292, bf16[2,11,32,128,128]{3,4,2,1,0:T(8,128)(2,1)} %get-tuple-element.255, f32[11,32,128,128]{3,2,1,0:T(8,128)} %fusion.293, f32[11,32,128,128]{3,2,1,0:T(8,128)} %fusion.295, f32[11,32,32,128]{3,2,1,0:T(8,128)} %copy-done), kind=kOutput, calls=%fused_computation.12.clone.1 | convolution fusion | flops 1175511040 | bytes 102236160 | tf_op jit(solution)/shard_map/while/body/eval_jaxpr/ckxb,xa->ckab/dot_general | solution.py:23
  846.6 5.8 fusion.294
  860.1 21.6 %fusion.293 = f32[11,32,128,128]{3,2,1,0:T(8,128)} fusion(f32[11,32,32,128]{3,2,1,0:T(8,128)S(1)} %convolution_add_fusion.4), kind=kOutput, calls=%fused_computation.58.clone.1 | convolution fusion | flops 1107353600 | bytes 28835840 | tf_op jit(solution)/shard_map/while/body/eval_jaxpr/ckxb,xa->ckab/dot_general | solution.py:23
  881.7 21.2 %fusion.292 = f32[11,32,128,128]{3,2,1,0:T(8,128)} fusion(f32[11,32,32,128]{3,2,1,0:T(8,128)S(1)} %convolution_add_fusion.4), kind=kOutput, calls=%fused_computation.48.clone.1 | convolution fusion | flops 1107353600 | bytes 28835840 | tf_op jit(solution)/shard_map/while/body/eval_jaxpr/ckxb,xa->ckab/dot_general | solution.py:23
  902.9 21.4 %fusion.295 = f32[11,32,128,128]{3,2,1,0:T(8,128)} fusion(f32[11,32,32,128]{3,2,1,0:T(8,128)S(1)} %convolution_subtract_fusion.4), kind=kOutput, calls=%fused_computation.50.clone.1 | convolution fusion | flops 1107353600 | bytes 28835840 | tf_op jit(solution)/shard_map/while/body/eval_jaxpr/ckxb,xa->ckab/dot_general | solution.py:23
  924.2 37.3 %fusion.296 = (f32[32,128,128]{1,2,0:T(8,128)}, f32[32,128,128]{1,2,0:T(8,128)S(1)}) fusion(f32[11,32,128,128]{3,2,1,0:T(8,128)} %fusion.292, bf16[2,11,32,128,128]{3,4,2,1,0:T(8,128)(2,1)} %get-tuple-element.255, f32[11,32,128,128]{3,2,1,0:T(8,128)} %fusion.293, f32[11,32,128,128]{3,2,1,0:T(8,128)} %fusion.295, f32[11,32,32,128]{3,2,1,0:T(8,128)} %copy-done), kind=kOutput, calls=%fused_computation.12.clone.1 | convolution fusion | flops 1175511040 | bytes 102236160 | tf_op jit(solution)/shard_map/while/body/eval_jaxpr/ckxb,xa->ckab/dot_general | solution.py:23
  994.7 6.3 all-to-all-start.1
  1001.0 9.0 slice_bitcast_fusion.3
  1010.0 7.7 pad_maximum_fusion
  1017.7 121.4 %all-to-all-done.1 = f32[6,32,128,128]{3,1,0,2:T(8,128)} async-done(((f32[6,32,128,128]{3,1,0,2:T(8,128)}), f32[6,32,128,128]{3,1,0,2:T(8,128)}, u32[]{:S(2)}, u32[]{:S(2)}) %all-to-all-start.1) | async-done | bytes 12582944 | tf_op jit(solution)/shard_map/all_to_all | solution.py:97
  1139.1 6.8 all-to-all-start
  1145.9 20.2 %copy.42 = f32[6,4,32,32,128]{4,3,2,1,0:T(8,128)} copy(f32[6,4,32,32,128]{4,2,0,3,1:T(8,128)} %bitcast.20) | data formatting | bytes 25165824 | tf_op jit(solution)/shard_map/all_to_all | solution.py:97
  1166.1 22.5 %fusion.134 = f32[6,32,128,128]{3,2,1,0:T(8,128)} fusion(f32[6,128,32,128]{3,2,1,0:T(8,128)} %bitcast.220), kind=kOutput, calls=%fused_computation.136 | convolution fusion | flops 2416148480 | bytes 25165824 | tf_op jit(solution)/shard_map/rkxy,kz->rxyz/dot_general | solution.py:23
  1188.5 95.5 %all-to-all-done = f32[4,6,32,32,128]{4,3,2,1,0:T(8,128)} async-done(((f32[4,6,32,32,128]{4,3,2,1,0:T(8,128)}), f32[4,6,32,32,128]{4,3,2,1,0:T(8,128)}, u32[]{:S(2)}, u32[]{:S(2)}) %all-to-all-start) | async-done | bytes 12582944 | tf_op jit(solution)/shard_map/all_to_all | solution.py:92
  1284.0 11.3 copy.38
  1295.3 24.5 %fusion.198 = (f32[6]{0:T(128)S(1)}, f32[6,32,128,128]{3,2,1,0:T(8,128)}) fusion(f32[6,32,128,128]{3,2,1,0:T(8,128)} %fusion.134, f32[6,128,32,128]{3,2,1,0:T(8,128)} %bitcast.219), kind=kOutput, calls=%fused_computation.210 | convolution fusion | flops 2425585664 | bytes 37748760 | tf_op jit(solution)/shard_map/rkxy,kz->rxyz/dot_general | solution.py:23
  1319.8 6.2 pmin.7
  (205 shorter events, 283.7 us)
Async XLA Ops:
  7.2 43.9 %all-gather.2.cloned.1.call-start = ((), (), s32[]{:S(2)}) async-start(), calls=%async_computation.2 | async-start | bytes 5406720 | tf_op jit(solution)/shard_map/all_gather | solution.py:46
  51.1 3.8 copy-start.2
  71.4 9.3 slice-start
  74.8 5.9 slice-start.1
  74.8 10.9 slice-start.2
  80.7 5.0 slice-start.3
  83.2 47.6 %copy-start = (f32[11,32,32,128]{3,2,1,0:T(8,128)}, f32[11,32,32,128]{3,2,1,0:T(8,128)S(1)}, u32[]{:S(2)}) copy-start(f32[11,32,32,128]{3,2,1,0:T(8,128)S(1)} %convolution_subtract_fusion.4) | copy-start | bytes 17301508 | tf_op jit(solution)/shard_map/while
  189.7 5.6 copy-start.1
  225.8 9.3 slice-start
  229.2 5.9 slice-start.1
  229.2 10.9 slice-start.2
  235.1 5.0 slice-start.3
  237.6 47.6 %copy-start = (f32[11,32,32,128]{3,2,1,0:T(8,128)}, f32[11,32,32,128]{3,2,1,0:T(8,128)S(1)}, u32[]{:S(2)}) copy-start(f32[11,32,32,128]{3,2,1,0:T(8,128)S(1)} %convolution_subtract_fusion.4) | copy-start | bytes 17301508 | tf_op jit(solution)/shard_map/while
  344.1 5.6 copy-start.1
  380.0 9.3 slice-start
  383.5 5.9 slice-start.1
  383.5 10.9 slice-start.2
  389.3 5.0 slice-start.3
  391.8 47.8 %copy-start = (f32[11,32,32,128]{3,2,1,0:T(8,128)}, f32[11,32,32,128]{3,2,1,0:T(8,128)S(1)}, u32[]{:S(2)}) copy-start(f32[11,32,32,128]{3,2,1,0:T(8,128)S(1)} %convolution_subtract_fusion.4) | copy-start | bytes 17301508 | tf_op jit(solution)/shard_map/while
  498.3 5.6 copy-start.1
  534.4 9.3 slice-start
  537.9 5.9 slice-start.1
  537.9 10.9 slice-start.2
  543.8 5.0 slice-start.3
  546.3 47.6 %copy-start = (f32[11,32,32,128]{3,2,1,0:T(8,128)}, f32[11,32,32,128]{3,2,1,0:T(8,128)S(1)}, u32[]{:S(2)}) copy-start(f32[11,32,32,128]{3,2,1,0:T(8,128)S(1)} %convolution_subtract_fusion.4) | copy-start | bytes 17301508 | tf_op jit(solution)/shard_map/while
  652.7 5.6 copy-start.1
  688.9 9.3 slice-start
  692.4 5.9 slice-start.1
  692.4 10.9 slice-start.2
  698.3 5.0 slice-start.3
  700.8 47.6 %copy-start = (f32[11,32,32,128]{3,2,1,0:T(8,128)}, f32[11,32,32,128]{3,2,1,0:T(8,128)S(1)}, u32[]{:S(2)}) copy-start(f32[11,32,32,128]{3,2,1,0:T(8,128)S(1)} %convolution_subtract_fusion.4) | copy-start | bytes 17301508 | tf_op jit(solution)/shard_map/while
  807.2 5.6 copy-start.1
  843.2 9.3 slice-start
  846.6 5.9 slice-start.1
  846.6 10.9 slice-start.2
  852.5 5.0 slice-start.3
  855.0 47.8 %copy-start = (f32[11,32,32,128]{3,2,1,0:T(8,128)}, f32[11,32,32,128]{3,2,1,0:T(8,128)S(1)}, u32[]{:S(2)}) copy-start(f32[11,32,32,128]{3,2,1,0:T(8,128)S(1)} %convolution_subtract_fusion.4) | copy-start | bytes 17301508 | tf_op jit(solution)/shard_map/while
  961.5 5.6 copy-start.1
  994.7 144.4 %all-to-all-start.1 = ((f32[6,32,128,128]{3,1,0,2:T(8,128)}), f32[6,32,128,128]{3,1,0,2:T(8,128)}, u32[]{:S(2)}, u32[]{:S(2)}) async-start(f32[6,32,128,128]{3,1,0,2:T(8,128)} %get-tuple-element.92), calls=%async_computation.1 | async-start | bytes 25165824 | tf_op jit(solution)/shard_map/all_to_all | solution.py:97
  1139.1 144.9 %all-to-all-start = ((f32[4,6,32,32,128]{4,3,2,1,0:T(8,128)}), f32[4,6,32,32,128]{4,3,2,1,0:T(8,128)}, u32[]{:S(2)}, u32[]{:S(2)}) async-start(f32[4,6,32,32,128]{4,3,2,1,0:T(8,128)} %pad_maximum_fusion), calls=%async_computation | async-start | bytes 25165824 | tf_op jit(solution)/shard_map/all_to_all | solution.py:92
Sparse Core Ops, SparseCore 0:
  13.1 37.9 all-gather.1
